TPU v7x, 256 devices: a whole 4x4x8 slice. The times are simulated.
256 devices in a mesh: span: 8 (over x, core), ulysses: 32 (over z, y).
Axes of the slice: x: 4, y: 4, z: 8, core: 2. Of those that a mesh axis runs over, the one named last changes fastest.
Arguments:
- query: bfloat16 [8, 1536, 4096], P('span', 'ulysses'), may hold values from -5 to 5
- keys_in: bfloat16 [8, 1536, 4096], P('span', 'ulysses'), may hold values from -5 to 5
- values_in: bfloat16 [8, 1536, 4096], P('span', 'ulysses'), may hold values from -6 to 6
- out_weight: bfloat16 [4096, 6144], P('ulysses'), may hold values from -0.75 to 0.75
- gate_table: bfloat16 [64, 6144], replicated, may hold values from 0.5 to 2
- levels: int32 [8], replicated, may hold values from 0 to 63
- first_visible: int32 [8], replicated, may hold values from 0 to 3, as said below
Outputs:
- update: bfloat16 [8, 1536, 6144], P('span', 'ulysses')
Inputs may be any that keep to these rules, and one draw needn't show every extreme that they name: first_visible[c] is at most c // 2 for span c; for the last span, whose index c is 7, it equals c // 2 exactly.
All inputs are finite; a program needn't handle non-finite values.
Results may differ from a plain program's by a relative error of at most 0.025.
Values may be sent and summed in bfloat16 or wider, within the bound.
A program may use at most 128 MiB of HBM per device.

v0:
```python
import jax
import jax.numpy as jnp
from jax import lax
from jax.sharding import PartitionSpec as P

HD = 128


def shards(query, keys_in, values_in, out_weight, gate_table, levels, first_visible):
    queries, key_heads, value_heads = (
        lax.all_to_all(query, "ulysses", split_axis=2, concat_axis=1, tiled=True),
        lax.all_to_all(keys_in, "ulysses", split_axis=2, concat_axis=1, tiled=True),
        lax.all_to_all(values_in, "ulysses", split_axis=2, concat_axis=1, tiled=True),
    )
    span_tok = queries.shape[1]
    width = queries.shape[2]
    heads = width // HD
    scale = 1.0 / HD**0.5
    span_now = lax.axis_index("span")
    first = first_visible[span_now]
    query_rows = queries[0].reshape(span_tok, heads, HD)

    def update_state(state, key_rows, value_rows):
        top, total, accum = state
        key_rows = key_rows.reshape(span_tok, heads, HD)
        value_rows = value_rows.reshape(span_tok, heads, HD)
        scores = (
            jnp.einsum("thd,shd->ths", query_rows, key_rows, preferred_element_type=jnp.float32)
            * scale
        )
        new_top = jnp.maximum(top, jnp.max(scores, axis=2))
        expo = jnp.exp(scores - new_top[:, :, None])
        shrink = jnp.exp(top - new_top)
        total = total * shrink + jnp.sum(expo, axis=2)
        summed = jnp.einsum(
            "ths,shd->thd",
            expo.astype(jnp.bfloat16),
            value_rows,
            preferred_element_type=jnp.float32,
        )
        accum = accum * shrink[:, :, None] + summed
        return (new_top, total, accum)

    start_state = (
        jnp.full((span_tok, heads), -jnp.inf, jnp.float32),
        jnp.zeros((span_tok, heads), jnp.float32),
        jnp.zeros((span_tok, heads, HD), jnp.float32),
    )
    state = start_state
    start = jnp.int32(0)
    key_piece = lax.all_gather(key_heads, "span", axis=0, tiled=True)
    value_piece = lax.all_gather(value_heads, "span", axis=0, tiled=True)
    for offset in range(key_piece.shape[0]):
        absorb_key_rows = key_piece[offset]
        absorb_value_rows = value_piece[offset]
        source = start + offset
        seen = (source >= first) & (source <= span_now)
        state = lax.cond(
            seen, lambda s: update_state(s, absorb_key_rows, absorb_value_rows), lambda s: s, state
        )
    top, total, accum = state
    attn = (accum / total[:, :, None]).reshape(span_tok, width).astype(jnp.bfloat16)
    projected = lax.psum_scatter(
        jnp.dot(attn, out_weight, preferred_element_type=jnp.float32).astype(jnp.bfloat16),
        "ulysses",
        scatter_dimension=0,
        tiled=True,
    ).astype(jnp.float32)
    selector = (jnp.arange(gate_table.shape[0], dtype=jnp.int32) == levels[span_now]).astype(
        jnp.bfloat16
    )
    gate = jnp.dot(selector[None, :], gate_table, preferred_element_type=jnp.float32)
    return (gate * projected).astype(jnp.bfloat16)[None]


def solution(mesh):
    placed = (
        P("span", "ulysses", None),
        P("span", "ulysses", None),
        P("span", "ulysses", None),
        P("ulysses", None),
        P(),
        P(),
        P(),
    )
    return jax.shard_map(
        shards, mesh=mesh, in_specs=placed, out_specs=P("span", "ulysses", None), check_vma=False
    )
```

profile of v0, /device:TPU:4, one launch (start us, length us, event | category | flops | bytes accessed | tf_op | source)
XLA Modules:
  0.0 497.4 jit_solution(356471984442059122)
XLA Ops:
  6.5 5.3 %copy.34 = bf16[1,48,4096]{1,0,2:T(2,128)(2,1)} copy(bf16[1,48,4096]{2,1,0:T(8,128)(2,1)} %param.24) | data formatting | bytes 786432 | tf_op args[1]
  12.4 23.4 %reduce.69 = bf16[4096,48]{1,0:T(8,128)(2,1)S(1)} reduce(bf16[4096,1,48]{2,1,0:T(2,128)(2,1)} %bitcast.430, bf16[]{:T(256)} %broadcast.139), dimensions={1}, to_apply=%bitcast.376.reduce_sub_computation | reduce | bytes 786434
  37.5 26.6 %all_to_all.51 = bf16[32,2,3072]{2,1,0:T(2,128)(2,1)S(1)} all-to-all(bf16[32,2,3072]{2,1,0:T(2,128)(2,1)S(1)} %reshape.285), channel_id=1, replica_groups=mesh['span'=8,'ulysses'=32] {'ulysses'}, dimensions={0} | all-to-all | bytes 786432 | tf_op jit(solution)/shard_map/all_to_all | solution.py:12
  64.1 4.1 reshape.286
  68.2 4.6 copy.35
  74.1 3.9 copy.40
  77.9 23.4 %reduce.71 = bf16[4096,48]{1,0:T(8,128)(2,1)S(1)} reduce(bf16[4096,1,48]{2,1,0:T(2,128)(2,1)} %bitcast.432, bf16[]{:T(256)} %broadcast.139), dimensions={1}, to_apply=%bitcast.380.reduce_sub_computation | reduce | bytes 786434
  103.0 18.8 %all_to_all.52 = bf16[32,2,3072]{2,1,0:T(2,128)(2,1)S(1)} all-to-all(bf16[32,2,3072]{2,1,0:T(2,128)(2,1)S(1)} %reshape.289), channel_id=1, replica_groups=mesh['span'=8,'ulysses'=32] {'ulysses'}, dimensions={0} | all-to-all | bytes 786432 | tf_op jit(solution)/shard_map/all_to_all | solution.py:13
  121.8 4.1 reshape.290
  125.9 4.6 copy.41
  131.5 5.2 %copy.37 = bf16[1,48,4096]{1,0,2:T(2,128)(2,1)} copy(bf16[1,48,4096]{2,1,0:T(8,128)(2,1)} %param.23) | data formatting | bytes 786432 | tf_op args[0]
  136.7 23.4 %reduce.70 = bf16[4096,48]{1,0:T(8,128)(2,1)S(1)} reduce(bf16[4096,1,48]{2,1,0:T(2,128)(2,1)} %bitcast.431, bf16[]{:T(256)} %broadcast.139), dimensions={1}, to_apply=%bitcast.378.reduce_sub_computation | reduce | bytes 786434
  162.6 4.3 all-to-all-start.1
  172.7 8.4 %all-to-all-done.1 = bf16[32,2,3072]{2,1,0:T(2,128)(2,1)S(1)} async-done(((bf16[32,2,3072]{2,1,0:T(2,128)(2,1)}), bf16[32,2,3072]{2,1,0:T(2,128)(2,1)S(1)}, u32[]{:S(2)}, u32[]{:S(2)}) %all-to-all-start.1) | async-done | bytes 393248 | tf_op jit(solution)/shard_map/all_to_all | solution.py:11
  181.2 4.1 reshape.288
  185.2 4.6 copy.38
  190.1 2.8 fusion.159
  192.9 2.9 fusion.158
  196.4 12.8 %conditional.10 = ((f32[1536,1]{0,1:T(1,128)S(1)}, f32[1536,1]{0,1:T(1,128)S(1)}, f32[1536,1,128]{2,0,1:T(8,128)S(1)})) conditional(s32[]{:T(128)} %convert_element_type.93, (f32[1536,1]{0,1:T(1,128)S(1)}, f32[1536,1]{0,1:T(1,128)S(1)}, f32[1536,1,128]{2,0,1:T(8,128)S(1)}) %get-tuple-element.333, (bf16[1,1536,128]{2,1,0:T(8,128)(2,1)}, ...), branch_computations={%region_8.0_spmd, %region_9.0_spmd} | conditional | flops 1222513152 | bytes 32741436 | solution.py:58
  209.2 5.9 %conditional.11 = ((f32[1536,1]{0,1:T(1,128)S(1)}, f32[1536,1]{0,1:T(1,128)S(1)}, f32[1536,1,128]{2,0,1:T(8,128)S(1)})) conditional(s32[]{:T(128)} %convert_element_type.92, (f32[1536,1]{0,1:T(1,128)S(1)}, f32[1536,1]{0,1:T(1,128)S(1)}, f32[1536,1,128]{2,0,1:T(8,128)S(1)}) %get-tuple-element.334, (bf16[1,1536,128]{2,1,0:T(8,128)(2,1)}, ...), branch_computations={%region_12.0_spmd, %region_13.0_spmd} | conditional | flops 1222513152 | bytes 32741436 | solution.py:58
  215.1 5.1 %conditional.12 = ((f32[1536,1]{0,1:T(1,128)S(1)}, f32[1536,1]{0,1:T(1,128)S(1)}, f32[1536,1,128]{2,0,1:T(8,128)S(1)})) conditional(s32[]{:T(128)} %convert_element_type.91, (f32[1536,1]{0,1:T(1,128)S(1)}, f32[1536,1]{0,1:T(1,128)S(1)}, f32[1536,1,128]{2,0,1:T(8,128)S(1)}) %get-tuple-element.335, (bf16[1,1536,128]{2,1,0:T(8,128)(2,1)S(1)}, ...), branch_computations={%region_16.0_spmd, %region_17.0_spmd} | conditional | flops 1222513152 | bytes 32741436 | solution.py:58
  222.4 2.8 conditional.15
  225.2 9.2 %convolution_convert_fusion = bf16[1536,6144]{1,0:T(8,128)(2,1)} fusion(bf16[128,6144]{1,0:T(8,128)(2,1)S(1)} %copy-done, f32[1536,1,128]{2,0,1:T(8,128)S(1)} %get-tuple-element.228, f32[1536]{0:T(1024)S(1)} %reduce.54), kind=kOutput, calls=%fused_computation.140 | convolution fusion | flops 2425749504 | bytes 21239808 | tf_op jit(solution)/shard_map/dot_general | solution.py:64
  236.5 251.9 %reduce-scatter.2.cloned.1.call-done = bf16[48,6144]{1,0:T(8,128)(2,1)} async-done(((bf16[1536,6144]{1,0:T(8,128)(2,1)}), bf16[48,6144]{1,0:T(8,128)(2,1)}) %reduce-scatter.2.cloned.1.call-update) | async-done | bytes 589840 | tf_op jit(solution)/shard_map/reduce_scatter | solution.py:63
  (67 shorter events, 32.9 us)
Async XLA Ops:
  6.5 218.7 %copy-start = (bf16[128,6144]{1,0:T(8,128)(2,1)S(1)}, bf16[128,6144]{1,0:T(8,128)(2,1)}, u32[]{:S(2)}) copy-start(bf16[128,6144]{1,0:T(8,128)(2,1)} %param.26) | copy-start | bytes 4718596
  6.5 67.5 %copy-start.7 = (bf16[1,48,4096]{2,1,0:T(8,128)(2,1)S(1)}, bf16[1,48,4096]{2,1,0:T(8,128)(2,1)}, u32[]{:S(2)}) copy-start(bf16[1,48,4096]{2,1,0:T(8,128)(2,1)} %param.25) | copy-start | bytes 1179652
  6.5 183.6 %all-gather.3.cloned.1.call-start = ((), (), s32[]{:S(2)}) async-start(), calls=%async_computation.4 | async-start | bytes 3538944 | tf_op jit(solution)/shard_map/all_gather | solution.py:51
  73.8 119.1 %all-gather.5.cloned.1.call-start = ((), (), s32[]{:S(2)}) async-start(), calls=%async_computation.5 | async-start | bytes 3538944 | tf_op jit(solution)/shard_map/all_gather | solution.py:52
  101.4 65.7 %copy-start.8 = (s32[8]{0:T(128)S(1)}, s32[8]{0:T(128)}, u32[]{:S(2)}) copy-start(s32[8]{0:T(128)} %param.29) | copy-start | bytes 100
  162.6 18.5 %all-to-all-start.1 = ((bf16[32,2,3072]{2,1,0:T(2,128)(2,1)}), bf16[32,2,3072]{2,1,0:T(2,128)(2,1)S(1)}, u32[]{:S(2)}, u32[]{:S(2)}) async-start(bf16[32,2,3072]{2,1,0:T(2,128)(2,1)} %reshape.287), calls=%async_computation.1 | async-start | bytes 786432 | tf_op jit(solution)/shard_map/all_to_all | solution.py:11
  167.0 321.5 %reduce-scatter.2.cloned.1.call-start = ((), (), s32[]{:S(2)}) async-start(), calls=%async_computation.6 | async-start | bytes 19464192 | tf_op jit(solution)/shard_map/reduce_scatter | solution.py:63
  203.3 3.9 copy-start.4
  209.2 3.9 copy-start.3
  215.4 2.8 copy-start.2
  234.4 0.7 copy-start.9
  234.4 1.2 copy-start.6
Sparse Core Ops, SparseCore 0:
  73.9 24.7 all-gather.2
  131.7 24.8 all-gather.4
  234.5 253.8 reduce-scatter.1
where the time goes:
time: 505 us; the launch traced here: 497 us
  waiting for transfers between devices  260 us (51%)
  other arithmetic  76.5 us (15%)
  local copies, waits for them, and re-layouts  56.5 us (11%)
  blocking collectives  45.4 us (9%)
  matrix products  22.4 us (4%)
  between operations  19 us (4%)
  loops' own time  12.7 us (3%)
    reduce_scatter x1, waiting for transfers between devices, shards(): lax.psum_scatter(jnp.dot(attn, out_weight, preferred_element_type=jnp.flo...  252 us
    unnamed x3, other arithmetic  70.3 us
    unnamed x23, local copies, waits for them, and re-layouts  33.7 us
    all_to_all x1, blocking collectives, shards(): lax.all_to_all(keys_in, 'ulysses', split_axis=2, concat_axis=1, tiled=True)  26.6 us
    all_to_all x1, blocking collectives, shards(): lax.all_to_all(values_in, 'ulysses', split_axis=2, concat_axis=1, tiled=T...  18.8 us
    another operation x8, loops' own time, shards(): lax.cond(seen, lambda s: update_state(s, absorb_key_rows, absorb_value_ro...  12.7 us
  transfers between devices with their start and end apart: 4, of which 2 were waited for; matrix products, arithmetic and copies ran while one was open for 17% of the time, Pallas kernels for 0%

commit v1 on v0

v1 whole, which is shorter than its diff:
```python
import functools
import math

import jax
import jax.numpy as jnp
from jax import lax
from jax.experimental import pallas as pl
from jax.experimental.pallas import tpu as pltpu
from jax.sharding import PartitionSpec as P

MESH = pl.DeviceIdType.MESH
f32, bf16 = jnp.float32, jnp.bfloat16

HD = 128
TOK = 1536
OWN = 48
Z, Y, X = 8, 4, 4
SLAB = 192
WIDE = 6144
COLS = WIDE // 8
HALF = 768
KC = 512
C = math.log2(math.e) / math.sqrt(HD)
LOW = -1e30


def remote(src, dst, send_sem, recv_sem, device):
    return pltpu.make_async_remote_copy(
        src_ref=src, dst_ref=dst, send_sem=send_sem, recv_sem=recv_sem, device_id=device, device_id_type=MESH
    )


def wait_bytes(ref, sem):
    pltpu.make_async_copy(ref, ref, sem).wait()


def kernel(
    q_in, k_in, v_in, w_in, gate_in, levels, first, out,
    qb, kb, vb, vt, po_s, po_r, ob, ag, wf, pb, rb,
    a2a_s, a2a_r, kx_s, kx_r, vx_s, vx_r, qx_s, qx_r, po_ss, po_rs, oz_s, oz_r, ag_s, ag_r, w_s, w_r, w_l, y_s, y_r,
):
    s, u = lax.axis_index("span"), lax.axis_index("ulysses")
    x, k = s // 2, s % 2
    z, y = u // Y, u % Y
    sib = x * 2 + (1 - k)

    barrier = pltpu.get_barrier_semaphore()

    def hail_ulysses(d, c):
        pl.semaphore_signal(barrier, inc=1, device_id=(s, (u + d) % 32), device_id_type=MESH)
        return c

    def hail_plane(d, c):
        pl.semaphore_signal(
            barrier, inc=1, device_id=((s + 1 + d // Y) % 8, z * Y + d % Y), device_id_type=MESH
        )
        return c

    lax.fori_loop(1, 32, hail_ulysses, 0)
    lax.fori_loop(0, 28, hail_plane, 0)
    w_local = pltpu.make_async_copy(
        w_in.at[:, pl.ds(pl.multiple_of(s * COLS, 128), COLS)],
        wf.at[pl.ds(pl.multiple_of(z * HD, 128), HD)],
        w_l,
    )
    w_local.start()
    pl.semaphore_wait(barrier, 59)

    mine = pl.ds(pl.multiple_of(u * OWN, 16), OWN)
    for i, (src, dst) in enumerate(((k_in, kb.at[x]), (v_in, vb.at[x]), (q_in, qb.at[k]))):

        def send_head(d, c, src=src, dst=dst, i=i):
            t = (u + d) % 32
            remote(
                src.at[:, pl.ds(pl.multiple_of(t * HD, 128), HD)], dst.at[mine], a2a_s.at[i], a2a_r.at[i], (s, t)
            ).start()
            return c

        lax.fori_loop(1, 32, send_head, 0)
        pltpu.make_async_copy(
            src.at[:, pl.ds(pl.multiple_of(u * HD, 128), HD)], dst.at[mine], a2a_r.at[i]
        ).start()

    level = levels[s]
    pick = (lax.broadcasted_iota(jnp.int32, (8, 64), 1) == level).astype(bf16)

    def to_chip(buf, slot, send_sem, recv_sem, chip):
        return remote(buf.at[slot], buf.at[slot], send_sem, recv_sem.at[slot], (chip * 2 + k, u))

    k_sends = {
        (0, 1): to_chip(kb, 0, kx_s.at[0], kx_r, 1),
        (0, 3): to_chip(kb, 0, kx_s.at[1], kx_r, 3),
        (1, 2): to_chip(kb, 1, kx_s.at[0], kx_r, 2),
        (1, 0): to_chip(kb, 1, kx_s.at[1], kx_r, 0),
        (2, 3): to_chip(kb, 2, kx_s.at[0], kx_r, 3),
    }
    k_relays = {
        (0, 3): to_chip(kb, 1, kx_s.at[2], kx_r, 3),
        (3, 2): to_chip(kb, 0, kx_s.at[2], kx_r, 2),
    }
    v_sends = {
        (0, 1): to_chip(vb, 0, vx_s.at[0], vx_r, 1),
        (0, 3): to_chip(vb, 0, vx_s.at[1], vx_r, 3),
        (1, 2): to_chip(vb, 1, vx_s.at[0], vx_r, 2),
        (2, 3): to_chip(vb, 2, vx_s.at[0], vx_r, 3),
    }
    v_relays = {
        (2, 3): to_chip(vb, 1, vx_s.at[2], vx_r, 3),
        (3, 2): to_chip(vb, 0, vx_s.at[2], vx_r, 2),
    }

    def start_all(copies):
        for (at, _), copy in copies.items():
            pl.when(x == at)(copy.start)

    def arrived(buf, sem, slot):
        wait_bytes(buf.at[slot], sem.at[slot])

    wait_bytes(kb.at[x], a2a_r.at[0])
    start_all(k_sends)
    pl.when(x == 0)(lambda: arrived(kb, kx_r, 1))
    pl.when(x == 3)(lambda: arrived(kb, kx_r, 0))
    start_all(k_relays)
    wait_bytes(vb.at[x], a2a_r.at[1])
    start_all(v_sends)
    pl.when(x == 2)(lambda: arrived(vb, vx_r, 1))
    pl.when(x == 3)(lambda: arrived(vb, vx_r, 0))
    start_all(v_relays)

    wait_bytes(qb.at[k], a2a_r.at[2])
    q_send = remote(qb.at[k], qb.at[k], qx_s, qx_r, (sib, u))
    q_send.start()

    w_local.wait()
    w_mine = pl.ds(pl.multiple_of(z * HD, 128), HD)

    def send_w(d, c):
        t = (z + d) % Z
        remote(wf.at[w_mine], wf.at[w_mine], w_s, w_r, (s, t * Y + y)).start()
        return c

    lax.fori_loop(1, Z, send_w, 0)

    pl.when(x == 1)(lambda: arrived(kb, kx_r, 0))
    pl.when(x == 1)(lambda: arrived(vb, vx_r, 0))
    for slot in (0, 1):
        pl.when(x == 2)(functools.partial(arrived, kb, kx_r, slot))
    pl.when(x == 2)(lambda: arrived(vb, vx_r, 0))
    for slot in (1, 2):
        pl.when(x == 3)(functools.partial(arrived, kb, kx_r, slot))
        pl.when(x == 3)(functools.partial(arrived, vb, vx_r, slot))

    def turn(i, c):
        vt[i] = vb[i].T
        return c

    lax.fori_loop(0, x + 1, turn, 0)

    def attend(which, span, half, low, count):
        q = qb[which, pl.ds(pl.multiple_of(half * HALF, 16), HALF)]
        start = first[span]

        def scores(chip, j):
            return lax.dot_general(
                kb[chip, pl.ds(j * KC, KC)], q, (((1,), (1,)), ((), ())), preferred_element_type=f32
            )

        def absorb(i, state):
            chip = low + count - 1 - i
            seen = 2 * chip + k >= start
            now = scores(chip, 0)
            for j in range(TOK // KC):
                later = scores(chip, j + 1) if j + 1 < TOK // KC else None
                top, total, accum = state
                new_top = jnp.maximum(top, jnp.where(seen, jnp.max(now, axis=0, keepdims=True), LOW))
                expo = jnp.exp2(now * C - jnp.where(seen, new_top * C, -LOW))
                shrink = jnp.exp2((top - new_top) * C)
                total = total * shrink + jnp.sum(expo, axis=0, keepdims=True)
                summed = jnp.dot(vt[chip, :, pl.ds(j * KC, KC)], expo.astype(bf16), preferred_element_type=f32)
                state = (new_top, total, accum * shrink + summed)
                now = later
            return state

        begin = (jnp.full((1, HALF), LOW, f32), jnp.zeros((1, HALF), f32), jnp.zeros((HD, HALF), f32))
        return lax.fori_loop(0, count, absorb, begin)

    wait_bytes(qb.at[1 - k], qx_r)

    last = x == 3
    sib_low = jnp.where(last & (k == 0), 2, 0)
    sib_count = x + 1 - k - sib_low
    own_low = jnp.where(last & (k == 1), 1, 0)
    own_count = x + 1 - own_low

    def give(half, c):
        top, total, accum = attend(1 - k, sib, half, sib_low, sib_count)
        po_s[half, pl.ds(0, HD)] = accum
        po_s[half, pl.ds(HD, 1)] = top
        po_s[half, pl.ds(HD + 1, 1)] = total
        remote(po_s.at[half], po_r.at[half], po_ss.at[half], po_rs.at[half], (sib, u)).start()
        return c

    lax.fori_loop(0, 2, give, 0)

    head_cols = pl.ds(pl.multiple_of(z * HD, 128), HD)

    def finish(half, c):
        top, total, accum = attend(k, s, half, own_low, own_count)
        wait_bytes(po_r.at[half], po_rs.at[half])
        top2 = po_r[half, pl.ds(HD, 1)]
        total2 = po_r[half, pl.ds(HD + 1, 1)]
        both = jnp.maximum(top, top2)
        one = jnp.exp2((top - both) * C)
        two = jnp.exp2((top2 - both) * C)
        inv = 1.0 / (total * one + total2 * two)
        attn = accum * (one * inv) + po_r[half, pl.ds(0, HD)] * (two * inv)
        ob[pl.ds(pl.multiple_of(half * HALF, 16), HALF)] = attn.T.astype(bf16)

        def send_slab(i, c):
            t = half * (Z // 2) + i
            rows = ob.at[pl.ds(pl.multiple_of(t * SLAB, 16), SLAB)]
            there = ag.at[s, :, head_cols]

            @pl.when(t != z)
            def _():
                remote(rows, there, oz_s, oz_r, (s, t * Y + y)).start()

            @pl.when(t == z)
            def _():
                pltpu.make_async_copy(rows, there, oz_r).start()

            return c

        lax.fori_loop(0, Z // 2, send_slab, 0)
        return c

    lax.fori_loop(0, 2, finish, 0)
    wait_bytes(ag.at[s], oz_r)

    def ag_copy(slot, i, to):
        return remote(ag.at[slot], ag.at[slot], ag_s.at[i], ag_r.at[slot], (to, u))

    ag_sends = [ag_copy(s, d - 1, ((x + d) % X) * 2 + k) for d in range(1, X)] + [ag_copy(s, 3, sib)]
    for copy in (ag_sends[0], ag_sends[2], ag_sends[1], ag_sends[3]):
        copy.start()

    wait_bytes(wf.at[pl.ds(0, 7 * HD)], w_r)

    def project(span):
        part = jnp.dot(ag[span], wf[...], preferred_element_type=f32).astype(bf16)
        pb[pl.ds(pl.multiple_of(span * SLAB, 16), SLAB)] = part
        there = rb.at[y, :, pl.ds(pl.multiple_of(s * COLS, 128), COLS)]

        def send_block(t, c):
            rows = pb.at[pl.ds(pl.multiple_of(span * SLAB + t * OWN, 16), OWN)]
            here = (span == s) & (t == y)

            @pl.when(here)
            def _():
                pltpu.make_async_copy(rows, there, y_r).start()

            @pl.when(jnp.logical_not(here))
            def _():
                remote(rows, there, y_s, y_r, (span, z * Y + t)).start()

            return c

        lax.fori_loop(0, Y, send_block, 0)

    project(s)
    wait_bytes(ag.at[sib], ag_r.at[sib])
    project(sib)
    relays = []
    for i, d in enumerate((1, 3, 2)):
        same = ((x + d) % X) * 2 + k
        wait_bytes(ag.at[same], ag_r.at[same])
        relay = ag_copy(same, 4 + i, sib)
        relay.start()
        relays.append(relay)
        project(same)
        other = ((x + d) % X) * 2 + 1 - k
        wait_bytes(ag.at[other], ag_r.at[other])
        project(other)

    gate = jnp.dot(pick, gate_in[...], preferred_element_type=f32)[0:1]
    wait_bytes(rb, y_r)
    total = rb[0].astype(f32)
    for i in range(1, Y):
        total = total + rb[i].astype(f32)
    out[...] = (gate * total).astype(bf16)

    for i, buf in enumerate((kb.at[x], vb.at[x], qb.at[k])):
        wait_bytes(buf.at[pl.ds(0, 31 * OWN)], a2a_s.at[i])
    for copies in (k_sends, k_relays, v_sends, v_relays):
        for (at, _), copy in copies.items():
            pl.when(x == at)(copy.wait_send)
    q_send.wait_send()
    for half in range(2):
        wait_bytes(po_s.at[half], po_ss.at[half])
    wait_bytes(ob.at[pl.ds(0, 7 * SLAB)], oz_s)
    wait_bytes(wf.at[pl.ds(0, 7 * HD)], w_s)
    for copy in ag_sends + relays:
        copy.wait_send()
    wait_bytes(pb.at[pl.ds(0, 31 * OWN)], y_s)


def shards(query, keys_in, values_in, out_weight, gate_table, levels, first_visible):
    vmem = pl.BlockSpec(memory_space=pltpu.VMEM)
    smem = pl.BlockSpec(memory_space=pltpu.SMEM)
    dma = pltpu.SemaphoreType.DMA
    out = pl.pallas_call(
        kernel,
        out_shape=jax.ShapeDtypeStruct((OWN, WIDE), bf16),
        in_specs=[vmem, vmem, vmem, pl.BlockSpec(memory_space=pl.ANY), vmem, smem, smem],
        out_specs=vmem,
        scratch_shapes=[
            pltpu.VMEM((2, TOK, HD), bf16),
            pltpu.VMEM((X, TOK, HD), bf16),
            pltpu.VMEM((X, TOK, HD), bf16),
            pltpu.VMEM((X, HD, TOK), bf16),
            pltpu.VMEM((2, HD + 8, HALF), f32),
            pltpu.VMEM((2, HD + 8, HALF), f32),
            pltpu.VMEM((TOK, HD), bf16),
            pltpu.VMEM((8, SLAB, Z * HD), bf16),
            pltpu.VMEM((Z * HD, COLS), bf16),
            pltpu.VMEM((8 * SLAB, COLS), bf16),
            pltpu.VMEM((Y, OWN, WIDE), bf16),
            dma((3,)), dma((3,)),
            dma((3,)), dma((X,)), dma((3,)), dma((X,)),
            dma, dma,
            dma((2,)), dma((2,)),
            dma, dma,
            dma((7,)), dma((8,)),
            dma, dma, dma,
            dma, dma,
        ],
        compiler_params=pltpu.CompilerParams(
            collective_id=0, has_side_effects=True, vmem_limit_bytes=56 * 2**20
        ),
    )(query[0], keys_in[0], values_in[0], out_weight, gate_table, levels, first_visible)
    return out[None]


def solution(mesh):
    placed = (
        P("span", "ulysses", None),
        P("span", "ulysses", None),
        P("span", "ulysses", None),
        P("ulysses", None),
        P(),
        P(),
        P(),
    )
    return jax.shard_map(
        shards, mesh=mesh, in_specs=placed, out_specs=P("span", "ulysses", None), check_vma=False
    )
```

time: 505 us -> 140 us (0.28)
  the two profiles are of different devices: /device:TPU:4 before, /device:TPU:155 now
where the time goes in v1:
time: 140 us; the launch traced here: 139 us
  Pallas kernels  138 us (99%)
  local copies, waits for them, and re-layouts  1.92 us (1%)
    pallas_call x1, Pallas kernels, shards(): pl.pallas_call(kernel, out_shape=jax.ShapeDtypeStruct((OWN, WIDE), bf16),...  138 us

profile of v1, /device:TPU:155, one launch (start us, length us, event | category | flops | bytes accessed | tf_op | source)
XLA Modules:
  0.0 139.4 jit_solution(15193757187843663477)
XLA Ops:
  0.0 137.5 %shard_map.73 = bf16[48,6144]{1,0:T(8,128)(2,1)} custom-call(bf16[48,4096]{1,0:T(8,128)(2,1)} %bitcast.5, bf16[48,4096]{1,0:T(8,128)(2,1)} %bitcast.6, bf16[48,4096]{1,0:T(8,128)(2,1)} %bitcast.7, bf16[128,6144]{1,0:T(8,128)(2,1)} %w_in.1, bf16[64,6144]{1,0:T(8,128)(2,1)} %gate_in.1, s32[8]{0:T(128)} %levels.1, s32[8]{0:T(128)} %first.1), custom_call_target="tpu_custom_call" | custom-call | tf_op jit(solution)/shard_map/pallas_call | solution.py:311
  137.5 1.9 %copy.9 = bf16[1,48,6144]{2,1,0:T(8,128)(2,1)} copy(bf16[1,48,6144]{2,1,0:T(8,128)(2,1)} %bitcast.4) | data formatting | bytes 1179648

commit v2 on v0

v2 whole, which is shorter than its diff:
```python
import functools
import math

import jax
import jax.numpy as jnp
from jax import lax
from jax.experimental import pallas as pl
from jax.experimental.pallas import tpu as pltpu
from jax.sharding import PartitionSpec as P

MESH = pl.DeviceIdType.MESH
f32, bf16 = jnp.float32, jnp.bfloat16

HD = 128
TOK = 1536
OWN = 48
Z, Y, X = 8, 4, 4
WIDE = 6144
COLS = WIDE // 8
PASS = 3
PTOK = TOK // PASS
POWN = OWN // PASS
SLAB = Y * POWN
KC = 512
C = math.log2(math.e) / math.sqrt(HD)
LOW = -1e30


def remote(src, dst, send_sem, recv_sem, device):
    return pltpu.make_async_remote_copy(
        src_ref=src, dst_ref=dst, send_sem=send_sem, recv_sem=recv_sem, device_id=device, device_id_type=MESH
    )


def wait_bytes(ref, sem):
    pltpu.make_async_copy(ref, ref, sem).wait()


def aligned(index, size, multiple):
    return pl.ds(pl.multiple_of(index * size, multiple), size)


def kernel(
    q_in, k_in, v_in, w_in, gate_in, levels, first, out,
    qb, kb, vb, vt, st, po_r, ob, ag, wf, gt, gs, pb, yb, xb,
    a2a_s, a2a_r, kx_s, kx_r, vx_s, vx_r, qx_s, qx_r, po_ss, po_rs, oz_s, oz_r, ag_s, ag_r,
    wl, wp_s, wp_r, wm_s, wm_r, y_s, y_r, x_s, x_r,
):
    s, u = lax.axis_index("span"), lax.axis_index("ulysses")
    x, k = s // 2, s % 2
    z, y = u // Y, u % Y
    sib = x * 2 + (1 - k)
    my_cols = aligned(s, COLS, 128)

    barrier = pltpu.get_barrier_semaphore()

    def hail_ulysses(d, c):
        pl.semaphore_signal(barrier, inc=1, device_id=(s, (u + d) % 32), device_id_type=MESH)
        return c

    def hail_span(d, c):
        pl.semaphore_signal(barrier, inc=1, device_id=((s + d) % 8, u), device_id_type=MESH)
        return c

    lax.fori_loop(1, 32, hail_ulysses, 0)
    lax.fori_loop(1, 8, hail_span, 0)
    w_local = pltpu.make_async_copy(w_in.at[:, my_cols], wf.at[aligned(z, HD, 128)], wl.at[0])
    w_local.start()
    g_local = pltpu.make_async_copy(gate_in.at[:, my_cols], gt, wl.at[1])
    g_local.start()
    pl.semaphore_wait(barrier, 38)

    mine = aligned(u, OWN, 16)
    mine_q = aligned(u, POWN, 16)
    moves = (
        (lambda t: k_in.at[:, aligned(t, HD, 128)], kb.at[x, mine]),
        (lambda t: v_in.at[:, aligned(t, HD, 128)], vb.at[x, mine]),
        (lambda t: q_in.at[:, :, aligned(t, HD, 128)], qb.at[:, k, mine_q]),
    )
    for i, (src, dst) in enumerate(moves):

        def send_head(d, c, src=src, dst=dst, i=i):
            t = (u + d) % 32
            remote(src(t), dst, a2a_s.at[i], a2a_r.at[i], (s, t)).start()
            return c

        lax.fori_loop(1, 32, send_head, 0)
        pltpu.make_async_copy(src(u), dst, a2a_r.at[i]).start()

    pick = jnp.zeros((8, 64), f32)
    rows8 = lax.broadcasted_iota(jnp.int32, (8, 64), 0)
    cols64 = lax.broadcasted_iota(jnp.int32, (8, 64), 1)
    for c in range(8):
        pick = jnp.where((rows8 == c) & (cols64 == levels[c]), 1.0, pick)
    g_local.wait()
    gs[...] = jnp.dot(pick.astype(bf16), gt[...], preferred_element_type=f32)

    st[:, :, 0:HD] = jnp.zeros((PASS, 2, HD, PTOK), f32)
    st[:, :, HD : HD + 1] = jnp.full((PASS, 2, 1, PTOK), LOW, f32)
    st[:, :, HD + 1 : HD + 2] = jnp.zeros((PASS, 2, 1, PTOK), f32)

    def along(buf, sends, recvs, slot, i, chip, j):
        part = buf.at[slot, pl.ds(j * KC, KC)]
        return remote(part, part, sends.at[i, j], recvs.at[slot, j], (chip * 2 + k, u))

    k_sends = ((0, 0, 0, 1), (0, 0, 1, 3), (1, 1, 0, 2), (1, 1, 1, 0), (2, 2, 0, 3))
    k_relays = ((0, 1, 2, 3), (3, 0, 2, 2))
    v_sends = ((0, 0, 0, 1), (0, 0, 1, 3), (1, 1, 0, 2), (2, 2, 0, 3))
    v_relays = ((2, 1, 2, 3), (1, 0, 2, 2))
    chunks = TOK // KC
    drains = []

    def start_chunk(buf, sends, recvs, entry, j):
        at, slot, i, chip = entry
        copy = along(buf, sends, recvs, slot, i, chip, j)
        pl.when(x == at)(copy.start)
        drains.append(lambda: pl.when(x == at)(copy.wait_send))

    def arrived(buf, recvs, slot, j):
        wait_bytes(buf.at[slot, pl.ds(j * KC, KC)], recvs.at[slot, j])

    def exchange(buf, sends, recvs, direct, relays):
        for j in range(chunks):
            for entry in direct:
                start_chunk(buf, sends, recvs, entry, j)
        for j in range(chunks):
            for entry in relays:
                pl.when(x == entry[0])(functools.partial(arrived, buf, recvs, entry[1], j))
                start_chunk(buf, sends, recvs, entry, j)

    def await_rest(wanted):
        for at, buf, recvs, slot in wanted:

            @pl.when(x == at)
            def _():
                for j in range(chunks):
                    arrived(buf, recvs, slot, j)

    def turn(chip, c):
        vt[chip] = vb[chip].T
        return c

    wait_bytes(kb.at[x], a2a_r.at[0])
    exchange(kb, kx_s, kx_r, k_sends, k_relays)
    wait_bytes(vb.at[x], a2a_r.at[1])
    exchange(vb, vx_s, vx_r, v_sends, v_relays)
    turn(x, 0)

    wait_bytes(qb.at[:, k], a2a_r.at[2])
    q_send = remote(qb.at[:, k], qb.at[:, k], qx_s, qx_r, (sib, u))
    q_send.start()

    def w_copies(t):
        up, down = (z + Z - t + 1) % Z, (z + t - 1) % Z
        size, shift = (HD, 0) if t < Z // 2 else (HD // 2, HD // 2)
        one = wf.at[pl.ds(pl.multiple_of(up * HD, 64), size)]
        two = wf.at[pl.ds(pl.multiple_of(down * HD + shift, 64), size)]
        i = t - 1
        return (
            remote(one, one, wp_s.at[i], wp_r.at[i], (s, (z + 1) % Z * Y + y)),
            remote(two, two, wm_s.at[i], wm_r.at[i], (s, (z + Z - 1) % Z * Y + y)),
        )

    def w_step(t):
        if t == 1:
            w_local.wait()
        else:
            for copy in w_copies(t - 1):
                copy.wait_recv()
        if t <= Z // 2:
            for copy in w_copies(t):
                copy.start()
                drains.append(copy.wait_send)

    w_step(1)

    even, odd = first[x * 2], first[x * 2 + 1]

    def absorb(q, chip, seen, state):
        def scores(j):
            return lax.dot_general(
                kb[chip, pl.ds(j * KC, KC)], q, (((1,), (1,)), ((), ())), preferred_element_type=f32
            )

        now = scores(0)
        for j in range(chunks):
            later = scores(j + 1) if j + 1 < chunks else None
            top, total, accum = state
            new_top = jnp.maximum(top, jnp.where(seen, jnp.max(now, axis=0, keepdims=True), LOW))
            expo = jnp.exp2(now * C - jnp.where(seen, new_top * C, -LOW))
            shrink = jnp.exp2((top - new_top) * C)
            total = total * shrink + jnp.sum(expo, axis=0, keepdims=True)
            summed = jnp.dot(vt[chip, :, pl.ds(j * KC, KC)], expo.astype(bf16), preferred_element_type=f32)
            state = (new_top, total, accum * shrink + summed)
            now = later
        return state

    def load(p, w):
        return st[p, w, pl.ds(HD, 1)], st[p, w, pl.ds(HD + 1, 1)], st[p, w, pl.ds(0, HD)]

    def store(p, w, state):
        top, total, accum = state
        st[p, w, pl.ds(0, HD)] = accum
        st[p, w, pl.ds(HD, 1)] = top
        st[p, w, pl.ds(HD + 1, 1)] = total

    def pair(p, low, high):
        @pl.when(high >= low)
        def _():
            q = qb[p].reshape(2 * PTOK, HD)
            which = lax.broadcasted_iota(jnp.int32, (1, 2 * PTOK), 1) // PTOK
            start = jnp.where(which == 0, even, odd)

            def step(i, state):
                chip = high - i
                return absorb(q, chip, 2 * chip + k >= start, state)

            state = tuple(jnp.concatenate(pieces, axis=1) for pieces in zip(load(p, 0), load(p, 1)))
            state = lax.fori_loop(0, high - low + 1, step, state)
            for w in range(2):
                store(p, w, tuple(piece[:, w * PTOK : (w + 1) * PTOK] for piece in state))

    def single(p, w, start, low, high):
        @pl.when(high >= low)
        def _():
            q = qb[p, w]

            def step(i, state):
                chip = high - i
                return absorb(q, chip, 2 * chip + k >= start, state)

            store(p, w, lax.fori_loop(0, high - low + 1, step, load(p, w)))

    share = [remote(st.at[p, 1 - k], po_r.at[p], po_ss.at[p], po_rs.at[p], (sib, u)) for p in range(PASS)]

    def near(p):
        single(p, 1, odd, x, jnp.where(k == 1, x, x - 1))
        pair(p, jnp.maximum(x - 1, 0), x - k)

    def far(p):
        chip = jnp.where(x == 3, 1, 0)
        pair(p, chip, jnp.where((x == 2) | ((x == 3) & (k == 1)), chip, -1))
        pl.when(k == 0)(share[p].start)
        single(p, 0, even, 0, jnp.where(x == 3, 1 - k, -1))
        pl.when(k == 1)(share[p].start)
        drains.append(share[p].wait_send)

    def finish(p):
        wait_bytes(po_r.at[p], po_rs.at[p])
        top, total, accum = load(p, k)
        top2, total2 = po_r[p, HD : HD + 1], po_r[p, HD + 1 : HD + 2]
        both = jnp.maximum(top, top2)
        one_s = jnp.exp2((top - both) * C)
        two_s = jnp.exp2((top2 - both) * C)
        inv = 1.0 / (total * one_s + total2 * two_s)
        attn = accum * (one_s * inv) + po_r[p, 0:HD] * (two_s * inv)
        ob[p] = attn.astype(bf16).T
        there = ag.at[p, s, :, aligned(z, HD, 128)]

        def send_slab(d, c):
            t = (z + d) % Z
            remote(ob.at[p, aligned(t, SLAB, 16)], there, oz_s.at[p], oz_r.at[p], (s, t * Y + y)).start()
            return c

        lax.fori_loop(1, Z, send_slab, 0)
        pltpu.make_async_copy(ob.at[p, aligned(z, SLAB, 16)], there, oz_r.at[p]).start()
        drains.append(lambda: wait_bytes(ob.at[p, pl.ds(0, (Z - 1) * SLAB)], oz_s.at[p]))

    def ag_copy(p, slot, i, to):
        return remote(ag.at[p, slot], ag.at[p, slot], ag_s.at[p, i], ag_r.at[p, slot], (to, u))

    def gather(p):
        wait_bytes(ag.at[p, s], oz_r.at[p])
        for i, to in enumerate([((x + d) % X) * 2 + k for d in (1, 3, 2)] + [sib]):
            copy = ag_copy(p, s, i, to)
            copy.start()
            drains.append(copy.wait_send)

    def pass_on(p):
        for i, d in enumerate((1, 3, 2)):
            slot = ((x + d) % X) * 2 + k
            wait_bytes(ag.at[p, slot], ag_r.at[p, slot])
            copy = ag_copy(p, slot, 4 + i, sib)
            copy.start()
            drains.append(copy.wait_send)

    def project(p):
        for d in range(X):
            slot = ((x + d) % X) * 2 + 1 - k
            wait_bytes(ag.at[p, slot], ag_r.at[p, slot])
        part = jnp.dot(ag[p].reshape(8 * SLAB, Z * HD), wf[...], preferred_element_type=f32)
        pb[p] = part.astype(bf16).reshape(8, Y, POWN, COLS)
        for i, d in enumerate((1, 3, 2)):
            t = (y + d) % Y
            copy = remote(pb.at[p, :, t], yb.at[p, y], y_s.at[p, i], y_r.at[p, y], (s, z * Y + t))
            copy.start()
            drains.append(copy.wait_send)

    def settle(p):
        total = pb[p, :, y].astype(f32)
        for d in (1, 3, 2):
            t = (y + d) % Y
            wait_bytes(yb.at[p, t], y_r.at[p, t])
            total = total + yb[p, t].astype(f32)
        xb[p] = (total * gs[...].reshape(8, 1, COLS)).astype(bf16)
        there = out.at[pl.ds(p * POWN, POWN), my_cols]
        for i in range(1, 8):
            t = (s + i) % 8
            copy = remote(xb.at[p, t], there, x_s.at[p, i - 1], x_r.at[p], (t, u))
            copy.start()
            drains.append(copy.wait_send)
        pltpu.make_async_copy(xb.at[p, s], there, x_r.at[p]).start()

    await_rest(((1, kb, kx_r, 0), (2, kb, kx_r, 1), (3, kb, kx_r, 2), (3, vb, vx_r, 2)))
    lax.fori_loop(jnp.maximum(x - 1, 0), x, turn, 0)
    wait_bytes(qb.at[:, 1 - k], qx_r)

    def late():
        await_rest(
            ((2, kb, kx_r, 0), (2, vb, vx_r, 0), (3, vb, vx_r, 0), (3, kb, kx_r, 1), (3, vb, vx_r, 1))
        )
        lax.fori_loop(0, jnp.maximum(x - 1, 0), turn, 0)

    near(0)
    w_step(2)
    near(1)
    late()
    far(0)
    w_step(3)
    far(1)
    finish(0)
    near(2)
    w_step(4)
    finish(1)
    gather(0)
    far(2)
    gather(1)
    w_step(5)
    finish(2)
    pass_on(0)
    project(0)
    pass_on(1)
    project(1)
    gather(2)
    settle(0)
    pass_on(2)
    project(2)
    settle(1)
    settle(2)
    for p in range(PASS):
        rows = out.at[pl.ds(p * POWN, POWN)]
        wait_bytes(rows, x_r.at[p])

    for i, buf in enumerate((kb.at[x], vb.at[x])):
        wait_bytes(buf.at[pl.ds(0, 31 * OWN)], a2a_s.at[i])
    wait_bytes(kb.at[x].at[pl.ds(0, 31 * OWN)], a2a_s.at[2])
    q_send.wait_send()
    for drain in drains:
        drain()


def shards(query, keys_in, values_in, out_weight, gate_table, levels, first_visible):
    anywhere = pl.BlockSpec(memory_space=pl.ANY)
    smem = pl.BlockSpec(memory_space=pltpu.SMEM)
    dma = pltpu.SemaphoreType.DMA
    vmem = pltpu.VMEM
    out = pl.pallas_call(
        kernel,
        out_shape=jax.ShapeDtypeStruct((OWN, WIDE), bf16),
        in_specs=[anywhere] * 5 + [smem, smem],
        out_specs=pl.BlockSpec(memory_space=pltpu.VMEM),
        scratch_shapes=[
            vmem((PASS, 2, PTOK, HD), bf16),
            vmem((X, TOK, HD), bf16),
            vmem((X, TOK, HD), bf16),
            vmem((X, HD, TOK), bf16),
            vmem((PASS, 2, HD + 8, PTOK), f32),
            vmem((PASS, HD + 8, PTOK), f32),
            vmem((PASS, PTOK, HD), bf16),
            vmem((PASS, 8, SLAB, Z * HD), bf16),
            vmem((Z * HD, COLS), bf16),
            vmem((64, COLS), bf16),
            vmem((8, COLS), f32),
            vmem((PASS, 8, Y, POWN, COLS), bf16),
            vmem((PASS, Y, 8, POWN, COLS), bf16),
            vmem((PASS, 8, POWN, COLS), bf16),
            dma((3,)), dma((3,)),
            dma((3, 3)), dma((X, 3)), dma((3, 3)), dma((X, 3)),
            dma, dma,
            dma((PASS,)), dma((PASS,)),
            dma((PASS,)), dma((PASS,)),
            dma((PASS, 7)), dma((PASS, 8)),
            dma((2,)), dma((4,)), dma((4,)), dma((4,)), dma((4,)),
            dma((PASS, 3)), dma((PASS, Y)),
            dma((PASS, 7)), dma((PASS,)),
        ],
        compiler_params=pltpu.CompilerParams(
            collective_id=0, has_side_effects=True, vmem_limit_bytes=56 * 2**20
        ),
    )(
        query.reshape(PASS, POWN, query.shape[2]), keys_in[0], values_in[0], out_weight, gate_table, levels,
        first_visible,
    )
    return out[None]


def solution(mesh):
    placed = (
        P("span", "ulysses", None),
        P("span", "ulysses", None),
        P("span", "ulysses", None),
        P("ulysses", None),
        P(),
        P(),
        P(),
    )
    return jax.shard_map(
        shards, mesh=mesh, in_specs=placed, out_specs=P("span", "ulysses", None), check_vma=False
    )
```

time: 505 us -> 115 us (0.23); the launches traced: 497 us -> 114 us
  waiting for transfers between devices: 260 us -> 0 us
  Pallas kernels: 0 us -> 112 us
  other arithmetic: 76.5 us -> 0 us
  local copies, waits for them, and re-layouts: 56.5 us -> 1.92 us
  blocking collectives: 45.4 us -> 0 us
  matrix products: 22.4 us -> 0 us
  between operations: 19 us -> 0.01 us
  loops' own time: 12.7 us -> 0 us
    reduce_scatter x1 -> x0, waiting for transfers between devices: 252 us -> none  [shards(): lax.psum_scatter(jnp.dot(attn, out_weight, preferred_element_type=jnp.flo...]
    pallas_call x0 -> x1, Pallas kernels: none -> 112 us  [shards(): pl.pallas_call(kernel, out_shape=jax.ShapeDtypeStruct((OWN, WIDE), bf16),...]
    unnamed x3 -> x0, other arithmetic: 70.3 us -> none
    all_to_all x2 -> x0, blocking collectives: 45.4 us -> none  [the longest x1 26.6 us: shards(): lax.all_to_all(keys_in, 'ulysses', split_axis=2, concat_axis=1, tiled=True)]
    unnamed x23 -> x1, local copies, waits for them, and re-layouts: 33.7 us -> 1.92 us
    dot_general x8 -> x0, matrix products: 22.4 us -> none  [the longest x1 9.17 us: shards(): jnp.dot(attn, out_weight, preferred_element_type=jnp.float32)]
    all_to_all x9 -> x0, local copies, waits for them, and re-layouts: 15.8 us -> none  [the longest x3 5.54 us: shards(): lax.all_to_all(values_in, 'ulysses', split_axis=2, concat_axis=1, tiled=T...]
    another operation x8 -> x0, loops' own time: 12.7 us -> none  [shards(): lax.cond(seen, lambda s: update_state(s, absorb_key_rows, absorb_value_ro...]
  transfers between devices with their start and end apart: 4 -> 0, of which waited for: 2 -> 0; matrix products, arithmetic and copies ran while one was open for 17% -> 0% of each run, Pallas kernels for 0% -> 0%
where the time goes in v2:
time: 115 us; the launch traced here: 114 us
  Pallas kernels  112 us (97%)
  local copies, waits for them, and re-layouts  1.92 us (2%)
    pallas_call x1, Pallas kernels, shards(): pl.pallas_call(kernel, out_shape=jax.ShapeDtypeStruct((OWN, WIDE), bf16),...  112 us

profile of v2, /device:TPU:4, one launch (start us, length us, event | category | flops | bytes accessed | tf_op | source)
XLA Modules:
  0.0 114.0 jit_solution(13899566364023003369)
XLA Ops:
  0.0 112.1 %shard_map.73 = bf16[48,6144]{1,0:T(8,128)(2,1)} custom-call(bf16[3,16,4096]{2,1,0:T(8,128)(2,1)} %bitcast.5, bf16[48,4096]{1,0:T(8,128)(2,1)} %bitcast.6, bf16[48,4096]{1,0:T(8,128)(2,1)} %bitcast.7, bf16[128,6144]{1,0:T(8,128)(2,1)} %w_in.1, bf16[64,6144]{1,0:T(8,128)(2,1)} %gate_in.1, s32[8]{0:T(128)} %levels.1, s32[8]{0:T(128)} %first.1), custom_call_target="tpu_custom_call" | custom-call | tf_op jit(solution)/shard_map/pallas_call | solution.py:367
  112.1 1.9 %copy.9 = bf16[1,48,6144]{2,1,0:T(8,128)(2,1)} copy(bf16[1,48,6144]{2,1,0:T(8,128)(2,1)} %bitcast.4) | data formatting | bytes 1179648

commit v3 on v2

--- a/solution.py
+++ b/solution.py
@@ -24,6 +24,7 @@
 KC = 512
 C = math.log2(math.e) / math.sqrt(HD)
 LOW = -1e30
+FIRST, LAST = slice(0, 4), slice(4, 8)
 
 
 def remote(src, dst, send_sem, recv_sem, device):
@@ -42,7 +43,7 @@
 
 def kernel(
     q_in, k_in, v_in, w_in, gate_in, levels, first, out,
-    qb, kb, vb, vt, st, po_r, ob, ag, wf, gt, gs, pb, yb, xb,
+    qb, kb, vb, vt, st, po_r, ob, ag, wf, gt, gs, pb, hb, cb, yb, xb,
     a2a_s, a2a_r, kx_s, kx_r, vx_s, vx_r, qx_s, qx_r, po_ss, po_rs, oz_s, oz_r, ag_s, ag_r,
     wl, wp_s, wp_r, wm_s, wm_r, y_s, y_r, x_s, x_r,
 ):
@@ -145,11 +146,6 @@
     wait_bytes(vb.at[x], a2a_r.at[1])
     exchange(vb, vx_s, vx_r, v_sends, v_relays)
     turn(x, 0)
-
-    wait_bytes(qb.at[:, k], a2a_r.at[2])
-    q_send = remote(qb.at[:, k], qb.at[:, k], qx_s, qx_r, (sib, u))
-    q_send.start()
-
     def w_copies(t):
         up, down = (z + Z - t + 1) % Z, (z + t - 1) % Z
         size, shift = (HD, 0) if t < Z // 2 else (HD // 2, HD // 2)
@@ -172,7 +168,12 @@
                 copy.start()
                 drains.append(copy.wait_send)
 
+
     w_step(1)
+
+    wait_bytes(qb.at[:, k], a2a_r.at[2])
+    q_send = remote(qb.at[:, k], qb.at[:, k], qx_s, qx_r, (sib, u))
+    q_send.start()
 
     even, odd = first[x * 2], first[x * 2 + 1]
 
@@ -266,6 +267,12 @@
         pltpu.make_async_copy(ob.at[p, aligned(z, SLAB, 16)], there, oz_r.at[p]).start()
         drains.append(lambda: wait_bytes(ob.at[p, pl.ds(0, (Z - 1) * SLAB)], oz_s.at[p]))
 
+    above, below = (y + 1) % Y, (y + Y - 1) % Y
+
+    def start(copy):
+        copy.start()
+        drains.append(copy.wait_send)
+
     def ag_copy(p, slot, i, to):
         return remote(ag.at[p, slot], ag.at[p, slot], ag_s.at[p, i], ag_r.at[p, slot], (to, u))
 
@@ -290,19 +297,25 @@
             wait_bytes(ag.at[p, slot], ag_r.at[p, slot])
         part = jnp.dot(ag[p].reshape(8 * SLAB, Z * HD), wf[...], preferred_element_type=f32)
         pb[p] = part.astype(bf16).reshape(8, Y, POWN, COLS)
-        for i, d in enumerate((1, 3, 2)):
-            t = (y + d) % Y
-            copy = remote(pb.at[p, :, t], yb.at[p, y], y_s.at[p, i], y_r.at[p, y], (s, z * Y + t))
-            copy.start()
-            drains.append(copy.wait_send)
+        for w, (t, far_spans, near_spans) in enumerate(((above, FIRST, LAST), (below, LAST, FIRST))):
+            opposite = (y + 2) % Y
+            start(remote(pb.at[p, far_spans, opposite], hb.at[p, w], y_s.at[p, w, 0], y_r.at[p, w, 0], (s, z * Y + t)))
+            start(remote(pb.at[p, near_spans, t], yb.at[p, w, 1], y_s.at[p, w, 1], y_r.at[p, w, 1], (s, z * Y + t)))
+
+    def forward(p):
+        for w, (t, far_spans) in enumerate(((above, FIRST), (below, LAST))):
+            wait_bytes(hb.at[p, w], y_r.at[p, w, 0])
+            both = hb[p, w].astype(f32) + pb[p, far_spans, t].astype(f32)
+            cb[p, w] = both.astype(bf16)
+            start(remote(cb.at[p, w], yb.at[p, w, 0], y_s.at[p, w, 2], y_r.at[p, w, 2], (s, z * Y + t)))
 
     def settle(p):
-        total = pb[p, :, y].astype(f32)
-        for d in (1, 3, 2):
-            t = (y + d) % Y
-            wait_bytes(yb.at[p, t], y_r.at[p, t])
-            total = total + yb[p, t].astype(f32)
-        xb[p] = (total * gs[...].reshape(8, 1, COLS)).astype(bf16)
+        for w in range(2):
+            wait_bytes(yb.at[p, w, 1], y_r.at[p, w, 1])
+            wait_bytes(yb.at[p, w, 0], y_r.at[p, w, 2])
+        for w, spans in enumerate((FIRST, LAST)):
+            total = pb[p, spans, y].astype(f32) + yb[p, w, 0].astype(f32) + yb[p, 1 - w, 1].astype(f32)
+            xb[p, spans] = (total * gs[spans].reshape(4, 1, COLS)).astype(bf16)
         there = out.at[pl.ds(p * POWN, POWN), my_cols]
         for i in range(1, 8):
             t = (s + i) % 8
@@ -339,13 +352,16 @@
     finish(2)
     pass_on(0)
     project(0)
+    gather(2)
     pass_on(1)
+    forward(0)
     project(1)
-    gather(2)
+    pass_on(2)
+    forward(1)
+    project(2)
     settle(0)
-    pass_on(2)
-    project(2)
     settle(1)
+    forward(2)
     settle(2)
     for p in range(PASS):
         rows = out.at[pl.ds(p * POWN, POWN)]
@@ -382,7 +398,9 @@
             vmem((64, COLS), bf16),
             vmem((8, COLS), f32),
             vmem((PASS, 8, Y, POWN, COLS), bf16),
-            vmem((PASS, Y, 8, POWN, COLS), bf16),
+            vmem((PASS, 2, 4, POWN, COLS), bf16),
+            vmem((PASS, 2, 4, POWN, COLS), bf16),
+            vmem((PASS, 2, 2, 4, POWN, COLS), bf16),
             vmem((PASS, 8, POWN, COLS), bf16),
             dma((3,)), dma((3,)),
             dma((3, 3)), dma((X, 3)), dma((3, 3)), dma((X, 3)),
@@ -391,7 +409,7 @@
             dma((PASS,)), dma((PASS,)),
             dma((PASS, 7)), dma((PASS, 8)),
             dma((2,)), dma((4,)), dma((4,)), dma((4,)), dma((4,)),
-            dma((PASS, 3)), dma((PASS, Y)),
+            dma((PASS, 2, 3)), dma((PASS, 2, 3)),
             dma((PASS, 7)), dma((PASS,)),
         ],
         compiler_params=pltpu.CompilerParams(

time: 115 us -> 109 us (0.948)
  Pallas kernels: 112 us -> 106 us
    pallas_call x1, Pallas kernels: 112 us -> 106 us  [shards(): pl.pallas_call(kernel, out_shape=jax.ShapeDtypeStruct((OWN, WIDE), bf16),...]
where the time goes in v3:
time: 109 us; the launch traced here: 108 us
  Pallas kernels  106 us (97%)
  local copies, waits for them, and re-layouts  1.92 us (2%)
    pallas_call x1, Pallas kernels, shards(): pl.pallas_call(kernel, out_shape=jax.ShapeDtypeStruct((OWN, WIDE), bf16),...  106 us

profile of v3, /device:TPU:4, one launch (start us, length us, event | category | flops | bytes accessed | tf_op | source)
XLA Modules:
  0.0 108.3 jit_solution(16174655184926870394)
XLA Ops:
  0.0 106.4 %shard_map.73 = bf16[48,6144]{1,0:T(8,128)(2,1)} custom-call(bf16[3,16,4096]{2,1,0:T(8,128)(2,1)} %bitcast.5, bf16[48,4096]{1,0:T(8,128)(2,1)} %bitcast.6, bf16[48,4096]{1,0:T(8,128)(2,1)} %bitcast.7, bf16[128,6144]{1,0:T(8,128)(2,1)} %w_in.1, bf16[64,6144]{1,0:T(8,128)(2,1)} %gate_in.1, s32[8]{0:T(128)} %levels.1, s32[8]{0:T(128)} %first.1), custom_call_target="tpu_custom_call" | custom-call | tf_op jit(solution)/shard_map/pallas_call | solution.py:383
  106.4 1.9 %copy.9 = bf16[1,48,6144]{2,1,0:T(8,128)(2,1)} copy(bf16[1,48,6144]{2,1,0:T(8,128)(2,1)} %bitcast.4) | data formatting | bytes 1179648

commit v4 on v3

--- a/solution.py
+++ b/solution.py
@@ -278,7 +278,7 @@
 
     def gather(p):
         wait_bytes(ag.at[p, s], oz_r.at[p])
-        for i, to in enumerate([((x + d) % X) * 2 + k for d in (1, 3, 2)] + [sib]):
+        for i, to in enumerate([((x + d) % X) * 2 + k for d in (2, 1, 3)] + [sib]):
             copy = ag_copy(p, s, i, to)
             copy.start()
             drains.append(copy.wait_send)
@@ -348,9 +348,9 @@
     gather(0)
     far(2)
     gather(1)
-    w_step(5)
     finish(2)
     pass_on(0)
+    w_step(5)
     project(0)
     gather(2)
     pass_on(1)

time: 109 us -> 110 us (level)
  no operation moved by 1% of the time
where the time goes in v4:
time: 110 us; the launch traced here: 109 us
  Pallas kernels  107 us (97%)
  local copies, waits for them, and re-layouts  1.92 us (2%)
    pallas_call x1, Pallas kernels, shards(): pl.pallas_call(kernel, out_shape=jax.ShapeDtypeStruct((OWN, WIDE), bf16),...  107 us

profile of v4, /device:TPU:4, one launch (start us, length us, event | category | flops | bytes accessed | tf_op | source)
XLA Modules:
  0.0 109.3 jit_solution(5015988869448825244)
XLA Ops:
  0.0 107.4 %shard_map.73 = bf16[48,6144]{1,0:T(8,128)(2,1)} custom-call(bf16[3,16,4096]{2,1,0:T(8,128)(2,1)} %bitcast.5, bf16[48,4096]{1,0:T(8,128)(2,1)} %bitcast.6, bf16[48,4096]{1,0:T(8,128)(2,1)} %bitcast.7, bf16[128,6144]{1,0:T(8,128)(2,1)} %w_in.1, bf16[64,6144]{1,0:T(8,128)(2,1)} %gate_in.1, s32[8]{0:T(128)} %levels.1, s32[8]{0:T(128)} %first.1), custom_call_target="tpu_custom_call" | custom-call | tf_op jit(solution)/shard_map/pallas_call | solution.py:383
  107.4 1.9 %copy.9 = bf16[1,48,6144]{2,1,0:T(8,128)(2,1)} copy(bf16[1,48,6144]{2,1,0:T(8,128)(2,1)} %bitcast.4) | data formatting | bytes 1179648
